TPU v7x, 256 devices: a whole 4x4x8 slice. The times are simulated.
256 devices in a mesh: blk: 8 (over y, x_lo), dp: 32 (over z, x_hi, core).
Axes of the slice: x: 4 (x_hi: 2, x_lo: 2; x = x_hi * 2 + x_lo), y: 4, z: 8, core: 2. Of those that a mesh axis runs over, the one named last changes fastest.
Arguments:
- images: bfloat16 [64, 32, 32, 640], P('dp', None, None, 'blk'), may hold values from -6 to 6
- out_grads: bfloat16 [64, 32, 32, 640], P('dp'), may hold values from -0.046875 to 0.046875
- patch_inverse: bfloat16 [5760, 5760], P('blk', 'dp'), may hold values from -0.5 to 4.5
- output_inverse: bfloat16 [640, 640], replicated, may hold values from -0.5 to 4.5
Outputs:
- preconditioned: float32 [640, 5760], P('dp', 'blk')
All inputs are finite; a program needn't handle non-finite values.
Results may differ from a plain program's by a relative error of at most 0.0065.
Values may be sent and summed in bfloat16 or wider, within the bound.
A program may use at most 128 MiB of HBM per device.

v0:
```python
import jax
import jax.numpy as jnp
from jax import lax
from jax.sharding import PartitionSpec as P


def patch_rows(images):
    padded = jnp.pad(images, ((0, 0), (1, 1), (1, 1), (0, 0)))
    height = images.shape[1]
    breadth = images.shape[2]
    shifted = [
        padded[:, row_tap : row_tap + height, col_tap : col_tap + breadth, :]
        for row_tap in range(3)
        for col_tap in range(3)
    ]
    stacked = jnp.stack(shifted, axis=-1)
    return stacked.reshape(-1, images.shape[3] * 9)


def on_device(images, out_grads, patch_inverse, output_inverse):
    patches = patch_rows(images)
    flat_grads = out_grads.reshape(-1, out_grads.shape[3])
    grad_slab = lax.dot_general(
        flat_grads, patches, (((0,), (0,)), ((), ())), preferred_element_type=jnp.float32
    ).astype(jnp.bfloat16)
    inverse_rows = lax.all_gather(patch_inverse, "dp", axis=1, tiled=True)
    applied = lax.dot_general(
        lax.all_gather(grad_slab, "blk", axis=1, tiled=True),
        inverse_rows,
        (((1,), (1,)), ((), ())),
        preferred_element_type=jnp.float32,
    )
    mixed = lax.dot_general(
        output_inverse.astype(jnp.float32),
        applied,
        (((0,), (0,)), ((), ())),
        precision=lax.Precision.HIGHEST,
        preferred_element_type=jnp.float32,
    )
    arrived = lax.all_to_all(mixed[None], "dp", split_axis=1, concat_axis=0, tiled=True)
    return jnp.sum(arrived, axis=0)


def solution(mesh):
    placed = (P("dp", None, None, "blk"), P("dp", None, None, None), P("blk", "dp"), P())
    return jax.shard_map(
        on_device, mesh=mesh, in_specs=placed, out_specs=P("dp", "blk"), check_vma=False
    )
```

profile of v0, /device:TPU:2, one launch (start us, length us, event | category | flops | bytes accessed | tf_op | source)
XLA Modules:
  0.0 364.7 jit_solution(6816475263785564952)
XLA Ops:
  6.5 0.0 copy-start
  6.5 0.0 copy-start.1
  6.5 0.0 all-gather.6.cloned.1.call-start
  6.5 0.7 all-gather.6.cloned.1.call-update
  7.3 0.0 all-gather.4.cloned.1.call-start
  7.3 2.1 fusion.2
  9.4 1.9 fusion.4
  11.4 2.0 fusion.6
  13.4 2.0 fusion.8
  15.4 0.0 copy-done.1
  15.4 0.8 bitcast_dynamic-update-slice_fusion
  16.2 1.0 fusion.10
  17.2 1.0 fusion.12
  18.2 0.9 fusion.14
  19.1 1.0 fusion.16
  20.1 13.7 %copy.7 = bf16[2,32,32,80,9]{2,1,0,4,3:T(8,128)(2,1)} copy(bf16[2,32,32,80,9]{3,2,1,0,4:T(8,128)(2,1)} %fusion.16) | data formatting | bytes 5898240 | tf_op jit(solution)/shard_map/stack | solution.py:16
  33.8 16.4 %reshape.9 = bf16[2048,720]{0,1:T(8,128)(2,1)} reshape(bf16[2,32,32,80,9]{2,1,0,4,3:T(8,128)(2,1)} %copy.7) | data formatting | bytes 5898240 | tf_op jit(solution)/shard_map/reshape | solution.py:17
  50.2 0.0 copy-done
  50.2 5.2 %fusion = bf16[640,720]{0,1:T(8,128)(2,1)} fusion(bf16[2048,720]{0,1:T(8,128)(2,1)} %reshape.9, bf16[2048,640]{1,0:T(8,128)(2,1)S(1)} %bitcast.54), kind=kOutput, calls=%fused_computation.2 | convolution fusion | flops 1887897600 | bytes 6492160 | tf_op jit(solution)/shard_map/dot_general | solution.py:23
  55.5 0.0 all-gather.4.cloned.1.call-update
  55.5 60.7 %all-gather.6.cloned.1.call-done = bf16[32,180,720]{2,1,0:T(8,128)(2,1)} async-done(((bf16[1,180,720]{2,1,0:T(8,128)(2,1)}), bf16[32,180,720]{2,1,0:T(8,128)(2,1)}) %all-gather.6.cloned.1.call-update) | async-done | bytes 8294416 | tf_op jit(solution)/shard_map/all_gather | solution.py:26
  116.2 13.4 %reshape.12 = bf16[5760,720]{1,0:T(8,128)(2,1)} reshape(bf16[32,180,720]{2,1,0:T(8,128)(2,1)} %all-gather.6.cloned.1.call-done) | data formatting | bytes 16588800
  129.6 0.0 copy-start.2
  129.6 137.9 %all-gather.4.cloned.1.call-done = bf16[640,5760]{0,1:T(8,128)(2,1)} async-done(((bf16[640,720]{0,1:T(8,128)(2,1)}), bf16[640,5760]{0,1:T(8,128)(2,1)}) %all-gather.4.cloned.1.call-update) | async-done | bytes 7372816 | tf_op jit(solution)/shard_map/all_gather | solution.py:28
  267.5 10.7 %fusion.17 = f32[640,720]{0,1:T(8,128)S(1)} fusion(bf16[640,5760]{0,1:T(8,128)(2,1)} %all-gather.4.cloned.1.call-done, bf16[5760,720]{1,0:T(8,128)(2,1)} %reshape.12), kind=kOutput, calls=%fused_computation.28 | convolution fusion | flops 5308416000 | bytes 17510400 | tf_op jit(solution)/shard_map/dot_general | solution.py:27
  278.1 0.0 copy-done.2
  278.1 3.8 %convolution_bitcast_fusion = f32[1,640,720]{1,2,0:T(8,128)} fusion(f32[640,720]{0,1:T(8,128)S(1)} %fusion.17, bf16[640,640]{1,0:T(8,128)(2,1)S(1)} %copy-done.2), kind=kOutput, calls=%fused_computation | convolution fusion | flops 3538944000 | bytes 4505600 | tf_op jit(solution)/shard_map/dot_general | solution.py:33
  282.0 5.1 %copy.8 = f32[1,640,720]{2,0,1:T(1,128)} copy(f32[1,640,720]{1,2,0:T(8,128)} %convolution_bitcast_fusion) | data formatting | bytes 3686400 | tf_op jit(solution)/shard_map/broadcast_in_dim | solution.py:40
  287.1 58.1 %all_to_all.12 = f32[1,640,720]{2,0,1:T(1,128)} all-to-all(f32[1,640,720]{2,0,1:T(1,128)} %copy.8), channel_id=1, replica_groups=mesh['blk'=8,'dp'=32] {'dp'}, dimensions={1} | all-to-all | bytes 3686400 | tf_op jit(solution)/shard_map/all_to_all | solution.py:40
  345.2 7.5 %reduce.2 = f32[640,720]{1,0:T(8,128)} reduce(f32[1,640,720]{2,0,1:T(1,128)} %all_to_all.12, f32[]{:T(128)} %constant.10), dimensions={0}, to_apply=%all_to_all.4.reduce_sub_computation | reduce | bytes 3686404 | tf_op jit(solution)/shard_map/all_to_all | solution.py:40
  352.7 2.7 all_to_all.10
  355.4 2.4 reduce_sum.9
Async XLA Ops:
  6.5 43.7 %copy-start = (bf16[2,32,32,640]{3,2,1,0:T(8,128)(2,1)S(1)}, bf16[2,32,32,640]{3,2,1,0:T(8,128)(2,1)}, u32[]{:S(2)}) copy-start(bf16[2,32,32,640]{3,2,1,0:T(8,128)(2,1)} %param.5) | copy-start | bytes 7864324
  6.5 8.9 %copy-start.1 = (bf16[2,32,32,80]{3,2,1,0:T(8,128)(2,1)S(1)}, bf16[2,32,32,80]{3,2,1,0:T(8,128)(2,1)}, u32[]{:S(2)}) copy-start(bf16[2,32,32,80]{3,2,1,0:T(8,128)(2,1)} %param.4) | copy-start | bytes 983044
  6.5 109.6 %all-gather.6.cloned.1.call-start = ((), (), s32[]{:S(2)}) async-start(), calls=%async_computation.2 | async-start | bytes 9326592 | tf_op jit(solution)/shard_map/all_gather | solution.py:26
  7.3 260.2 %all-gather.4.cloned.1.call-start = ((), (), s32[]{:S(2)}) async-start(), calls=%async_computation.1 | async-start | bytes 8294400 | tf_op jit(solution)/shard_map/all_gather | solution.py:28
  129.6 148.5 %copy-start.2 = (bf16[640,640]{1,0:T(8,128)(2,1)S(1)}, bf16[640,640]{1,0:T(8,128)(2,1)}, u32[]{:S(2)}) copy-start(bf16[640,640]{1,0:T(8,128)(2,1)} %param.7) | copy-start | bytes 2457604
Sparse Core Ops, SparseCore 0:
  10.1 106.0 all-gather.5
  118.0 149.4 all-gather.3
where the time goes:
time: 367 us; the launch traced here: 365 us
  waiting for transfers between devices  199 us (54%)
  local copies, waits for them, and re-layouts  64.2 us (17%)
  blocking collectives  58.1 us (16%)
  matrix products  19.7 us (5%)
  between operations  13.4 us (4%)
  other arithmetic  9.98 us (3%)
    all_gather x1, waiting for transfers between devices, on_device(): lax.all_gather(grad_slab, 'blk', axis=1, tiled=True)  138 us
    all_gather x1, waiting for transfers between devices, on_device(): inverse_rows = lax.all_gather(patch_inverse, 'dp', axis=1, tiled=True)  60.7 us
    all_to_all x1, blocking collectives, on_device(): lax.all_to_all(mixed[None], 'dp', split_axis=1, concat_axis=0, tiled=True)  58.1 us
    unnamed x15, local copies, waits for them, and re-layouts  25.2 us
    reshape x1, local copies, waits for them, and re-layouts, patch_rows(): return stacked.reshape(-1, images.shape[3] * 9)  16.4 us
    another operation x2, local copies, waits for them, and re-layouts, patch_rows(): stacked = jnp.stack(shifted, axis=-1)  14.7 us
    dot_general x1, matrix products, on_device(): lax.dot_general(lax.all_gather(grad_slab, 'blk', axis=1, tiled=True), inv...  10.7 us
    all_to_all x1, other arithmetic, on_device(): lax.all_to_all(mixed[None], 'dp', split_axis=1, concat_axis=0, tiled=True)  7.55 us
  transfers between devices with their start and end apart: 2, of which 2 were waited for; matrix products, arithmetic and copies ran while one was open for 17% of the time, Pallas kernels for 0%

commit v1 on v0

v1 whole, which is shorter than its diff:
```python
import functools

import jax
import jax.numpy as jnp
from jax import lax
from jax.experimental import pallas as pl
from jax.experimental.pallas import tpu as pltpu
from jax.sharding import PartitionSpec as P

MESH = pl.DeviceIdType.MESH
BF = jnp.bfloat16
F32 = jnp.float32


def dot(a, b, dims):
    return lax.dot_general(a, b, (dims, ((), ())), preferred_element_type=F32)


def kernel(
    img_h, g_h, p_h, o_h, out_ref,
    img_v, g_v, o_v, pbuf, patches, t_v, sp, dbuf, ssum, rbuf, hbuf, hmat, pcat, acc, pk, pr, fin,
    load_sem, p_send, p_recv, d_send, d_recv, rs_send, rs_recv, ag_send, ag_recv, pl_send, pl_recv, t_send, t_recv,
):
    blk = lax.axis_index("blk")
    dp = lax.axis_index("dp")
    core = dp % 2
    pos = dp // 2
    x_hi = pos % 2
    z = dp // 4
    quarter = core * 2 + x_hi
    sibling = {"blk": blk, "dp": dp + 1 - 2 * core}
    partner = {"blk": blk, "dp": dp + 2 - 4 * x_hi}
    to_blk, to_dp = z, 8 * quarter + blk
    from_blk = dp % 8
    from_quarter = dp // 8
    from_dp = blk * 4 + (from_quarter % 2) * 2 + from_quarter // 2
    stays = jnp.logical_and(to_blk == blk, to_dp == dp)

    loads = [
        pltpu.make_async_copy(img_h, img_v, load_sem.at[0]),
        pltpu.make_async_copy(p_h, pbuf.at[dp % 4], load_sem.at[1]),
        pltpu.make_async_copy(g_h, g_v, load_sem.at[2]),
        pltpu.make_async_copy(o_h, o_v, load_sem.at[3]),
    ]
    for load in loads:
        load.start()

    barrier = pltpu.get_barrier_semaphore()
    pl.semaphore_signal(barrier, inc=1, device_id=sibling, device_id_type=MESH)
    for j in range(1, 16):
        pl.semaphore_signal(
            barrier, inc=1, device_id={"blk": blk, "dp": ((pos + j) % 16) * 2 + core}, device_id_type=MESH
        )
    for j in range(1, 8):
        pl.semaphore_signal(barrier, inc=1, device_id={"blk": (blk + j) % 8, "dp": dp}, device_id_type=MESH)

    @pl.when(jnp.logical_not(stays))
    def _():
        pl.semaphore_signal(barrier, inc=1, device_id={"blk": from_blk, "dp": from_dp}, device_id_type=MESH)

    loads[0].wait()
    eye = (
        lax.broadcasted_iota(jnp.int32, (80, 80), 0) == lax.broadcasted_iota(jnp.int32, (80, 80), 1)
    ).astype(F32).astype(BF)
    img_t = dot(eye, img_v[...], ((1,), (1,)))
    lane = lax.broadcasted_iota(jnp.int32, (80, 2048), 1)
    col = lane & 31
    row = (lane >> 5) & 31
    zero = jnp.zeros((80, 2048), F32)
    for kw in range(3):
        if kw == 0:
            shifted = jnp.where(col == 0, zero, pltpu.roll(img_t, 1, 1))
        elif kw == 1:
            shifted = img_t
        else:
            shifted = jnp.where(col == 31, zero, pltpu.roll(img_t, 2047, 1))
        for kh in range(3):
            if kh == 0:
                piece = jnp.where(row == 0, zero, pltpu.roll(shifted, 32, 1))
            elif kh == 1:
                piece = shifted
            else:
                piece = jnp.where(row == 31, zero, pltpu.roll(shifted, 2016, 1))
            tap = kh * 3 + kw
            patches[80 * tap : 80 * tap + 80, :] = piece.astype(BF)

    pl.semaphore_wait(barrier, 23 + jnp.where(stays, 0, 1))
    loads[1].wait()
    mine = dp % 4
    theirs = (mine + 2) % 4

    def p_copy(slot, index, target):
        return pltpu.make_async_remote_copy(
            src_ref=pbuf.at[slot], dst_ref=pbuf.at[slot], send_sem=p_send.at[index], recv_sem=p_recv.at[index],
            device_id=target, device_id_type=MESH,
        )

    p_out = p_copy(mine, 0, partner)
    p_side = p_copy(mine, 1, sibling)
    p_out.start()
    p_side.start()

    loads[2].wait()
    t_v[0:720, :] = dot(patches[...], g_v[...], ((1,), (0,))).astype(BF)
    t_v[720:768, :] = jnp.zeros((48, 640), BF)
    loads[3].wait()
    for owner in range(2):
        for half in range(2):
            rows = 160 * (2 * owner + half)
            mixed = dot(o_v[rows : rows + 160, :], t_v[...], ((1,), (1,))).astype(BF)
            for k in range(8):
                sp[owner, 2 * k + half, :, 0:768] = mixed[16 * k : 16 * k + 16, :]
            for k in range(6):
                top = 128 + 16 * (k // 3)
                left = 256 * (k % 3)
                sp[owner, 2 * k + half, :, 768:1024] = mixed[top : top + 16, left : left + 256]
            for k in range(6, 8):
                sp[owner, 2 * k + half, :, 768:1024] = jnp.zeros((16, 256), BF)

    d_copy = pltpu.make_async_remote_copy(
        src_ref=sp.at[1 - core], dst_ref=dbuf, send_sem=d_send, recv_sem=d_recv,
        device_id=sibling, device_id_type=MESH,
    )
    d_copy.start()
    p_out.wait_recv()
    p_fwd = p_copy(theirs, 2, sibling)
    p_fwd.start()
    d_copy.wait_recv()
    ssum[...] = (sp[core].astype(F32) + dbuf[...].astype(F32)).astype(BF)

    rs = []
    for j in range(1, 16):
        peer = (pos + j) % 16
        rs.append(
            pltpu.make_async_remote_copy(
                src_ref=ssum.at[peer], dst_ref=rbuf.at[j], send_sem=rs_send.at[j], recv_sem=rs_recv.at[j],
                device_id={"blk": blk, "dp": peer * 2 + core}, device_id_type=MESH,
            )
        )
    for copy in rs:
        copy.start()

    p_side.wait_recv()
    p_fwd.wait_recv()
    prow = lax.broadcasted_iota(jnp.int32, (768, 720), 0)
    pcol = lax.broadcasted_iota(jnp.int32, (768, 720), 1)
    tap = (prow * 52429) >> 22
    wanted = jnp.where(prow < 720, (prow - 80 * tap) * 9 + tap, -1)
    order = (pcol == wanted).astype(F32).astype(BF)
    side_by_side = jnp.concatenate([dot(order, pbuf[s], ((1,), (0,))) for s in range(4)], axis=1)
    pcat[...] = side_by_side.astype(BF)

    for copy in rs:
        copy.wait_recv()
    total = ssum[pos].astype(F32)
    for j in range(1, 16):
        total = total + rbuf[j].astype(F32)
    hbuf[z] = total.astype(BF)

    ag = []
    for j in range(1, 8):
        peer = (z + j) % 8
        ag.append(
            pltpu.make_async_remote_copy(
                src_ref=hbuf.at[z], dst_ref=hbuf.at[z], send_sem=ag_send.at[j], recv_sem=ag_recv.at[j],
                device_id={"blk": blk, "dp": peer * 4 + x_hi * 2 + core}, device_id_type=MESH,
            )
        )
    for copy in ag:
        copy.start()
    for copy in ag:
        copy.wait_recv()
    for k in range(8):
        hmat[16 * k : 16 * k + 16, :] = hbuf[k, :, 0:768]
    for k in range(6):
        top = 128 + 16 * (k // 3)
        left = 256 * (k % 3)
        hmat[top : top + 16, left : left + 256] = hbuf[k, :, 768:1024]
    acc[:, 0:720] = dot(hmat[...], pcat[...], ((1,), (0,)))
    acc[:, 720:768] = jnp.zeros((160, 48), F32)

    for k in range(8):
        pk[k, :, 0:768] = acc[20 * k : 20 * k + 16, :].astype(BF)
        tail = acc[20 * k + 16 : 20 * k + 20, :]
        pieces = [tail[:, 0:256], tail[:, 256:512], tail[:, 512:768], jnp.zeros((4, 256), F32)]
        pk[k, :, 768:1024] = jnp.concatenate(pieces, axis=0).astype(BF)
    plane = []
    for j in range(1, 8):
        peer = (blk + j) % 8
        plane.append(
            pltpu.make_async_remote_copy(
                src_ref=pk.at[peer], dst_ref=pr.at[j], send_sem=pl_send.at[j], recv_sem=pl_recv.at[j],
                device_id={"blk": peer, "dp": dp}, device_id_type=MESH,
            )
        )
    for copy in plane:
        copy.start()
    for copy in plane:
        copy.wait_recv()
    total = pk[blk].astype(F32)
    for j in range(1, 8):
        total = total + pr[j].astype(F32)
    fin[0:16, :] = total[:, 0:720]
    fin[16:20, 0:256] = total[0:4, 768:1024]
    fin[16:20, 256:512] = total[4:8, 768:1024]
    fin[16:20, 512:720] = total[8:12, 768:976]

    def last():
        return pltpu.make_async_remote_copy(
            src_ref=fin, dst_ref=out_ref, send_sem=t_send, recv_sem=t_recv,
            device_id={"blk": to_blk, "dp": to_dp}, device_id_type=MESH,
        )

    @pl.when(stays)
    def _():
        copy = pltpu.make_async_copy(fin, out_ref, t_send)
        copy.start()
        copy.wait()

    @pl.when(jnp.logical_not(stays))
    def _():
        copy = last()
        copy.start()
        copy.wait_recv()
        copy.wait_send()

    p_out.wait_send()
    p_side.wait_send()
    p_fwd.wait_send()
    d_copy.wait_send()
    for copy in rs + ag + plane:
        copy.wait_send()


def on_device(images, out_grads, patch_inverse, output_inverse):
    dma = pltpu.SemaphoreType.DMA
    return pl.pallas_call(
        kernel,
        out_shape=jax.ShapeDtypeStruct((20, 720), F32),
        in_specs=[pl.BlockSpec(memory_space=pl.ANY)] * 4,
        out_specs=pl.BlockSpec(memory_space=pltpu.VMEM),
        scratch_shapes=[
            pltpu.VMEM((2048, 80), BF),
            pltpu.VMEM((2048, 640), BF),
            pltpu.VMEM((640, 640), BF),
            pltpu.VMEM((4, 720, 180), BF),
            pltpu.VMEM((720, 2048), BF),
            pltpu.VMEM((768, 640), BF),
            pltpu.VMEM((2, 16, 16, 1024), BF),
            pltpu.VMEM((16, 16, 1024), BF),
            pltpu.VMEM((16, 16, 1024), BF),
            pltpu.VMEM((16, 16, 1024), BF),
            pltpu.VMEM((8, 16, 1024), BF),
            pltpu.VMEM((160, 768), BF),
            pltpu.VMEM((768, 720), BF),
            pltpu.VMEM((160, 768), F32),
            pltpu.VMEM((8, 16, 1024), BF),
            pltpu.VMEM((8, 16, 1024), BF),
            pltpu.VMEM((20, 720), F32),
            dma((4,)),
            dma((3,)), dma((3,)),
            dma, dma,
            dma((16,)), dma((16,)),
            dma((8,)), dma((8,)),
            dma((8,)), dma((8,)),
            dma, dma,
        ],
        compiler_params=pltpu.CompilerParams(
            collective_id=0, has_side_effects=True, vmem_limit_bytes=48 * 1024 * 1024
        ),
        cost_estimate=pl.CostEstimate(flops=3 * 10**9, bytes_accessed=5 * 10**6, transcendentals=0),
    )(
        images.reshape(2048, 80),
        out_grads.reshape(2048, 640),
        patch_inverse,
        output_inverse,
    )


def solution(mesh):
    placed = (P("dp", None, None, "blk"), P("dp", None, None, None), P("blk", "dp"), P())
    return jax.shard_map(
        on_device, mesh=mesh, in_specs=placed, out_specs=P("dp", "blk"), check_vma=False
    )
```

time: 367 us -> 64.3 us (0.18)
  the two profiles are of different devices: /device:TPU:2 before, /device:TPU:37 now
where the time goes in v1:
time: 64.3 us; the launch traced here: 64.1 us
  Pallas kernels  58.4 us (91%)
  local copies, waits for them, and re-layouts  5.68 us (9%)
    pallas_call x1, Pallas kernels, on_device(): pl.pallas_call(kernel, out_shape=jax.ShapeDtypeStruct((20, 720), F32), in...  58.4 us
    unnamed x8, local copies, waits for them, and re-layouts  5.68 us

profile of v1, /device:TPU:37, one launch (start us, length us, event | category | flops | bytes accessed | tf_op | source)
XLA Modules:
  0.0 64.1 jit_solution(2288181560859715745)
XLA Ops:
  0.0 1.1 %copy.5.p_h = bf16[720,180]{1,0:T(8,128)(2,1)S(1)} copy(bf16[720,180]{0,1:T(8,128)(2,1)} %param.6) | data formatting | bytes 518400 | tf_op args[2]
  1.1 0.0 copy-start
  1.1 1.7 %copy-done = bf16[2,32,32,640]{3,2,1,0:T(8,128)(2,1)S(1)} copy-done((bf16[2,32,32,640]{3,2,1,0:T(8,128)(2,1)S(1)}, bf16[2,32,32,640]{3,2,1,0:T(8,128)(2,1)}, u32[]{:S(2)}) %copy-start) | copy-done | bytes 2621464
  2.9 0.0 copy-start.1
  2.9 1.1 %copy-done.1 = bf16[640,640]{1,0:T(8,128)(2,1)S(1)} copy-done((bf16[640,640]{1,0:T(8,128)(2,1)S(1)}, bf16[640,640]{1,0:T(8,128)(2,1)}, u32[]{:S(2)}) %copy-start.1) | copy-done | bytes 819224
  4.0 0.0 copy-start.2
  4.0 1.0 %copy-done.2 = bf16[2,32,32,80]{3,2,1,0:T(8,128)(2,1)S(1)} copy-done((bf16[2,32,32,80]{3,2,1,0:T(8,128)(2,1)S(1)}, bf16[2,32,32,80]{3,2,1,0:T(8,128)(2,1)}, u32[]{:S(2)}) %copy-start.2) | copy-done | bytes 327704
  5.1 58.4 %shard_map.46 = f32[20,720]{1,0:T(8,128)S(1)} custom-call(bf16[2048,80]{1,0:T(8,128)(2,1)S(1)} %bitcast.3, bf16[2048,640]{1,0:T(8,128)(2,1)S(1)} %bitcast.2, bf16[720,180]{1,0:T(8,128)(2,1)S(1)} %copy.5.p_h, bf16[640,640]{1,0:T(8,128)(2,1)S(1)} %copy-done.1), custom_call_target="tpu_custom_call" | custom-call | flops 3000000000 | bytes 5000000 | tf_op jit(solution)/shard_map/pallas_call | solution.py:237
  63.4 0.6 copy.7
Async XLA Ops:
  1.1 1.7 %copy-start = (bf16[2,32,32,640]{3,2,1,0:T(8,128)(2,1)S(1)}, bf16[2,32,32,640]{3,2,1,0:T(8,128)(2,1)}, u32[]{:S(2)}) copy-start(bf16[2,32,32,640]{3,2,1,0:T(8,128)(2,1)} %param.5) | copy-start | bytes 7864324
  2.9 1.1 %copy-start.1 = (bf16[640,640]{1,0:T(8,128)(2,1)S(1)}, bf16[640,640]{1,0:T(8,128)(2,1)}, u32[]{:S(2)}) copy-start(bf16[640,640]{1,0:T(8,128)(2,1)} %o_h.1) | copy-start | bytes 2457604
  4.0 1.0 %copy-start.2 = (bf16[2,32,32,80]{3,2,1,0:T(8,128)(2,1)S(1)}, bf16[2,32,32,80]{3,2,1,0:T(8,128)(2,1)}, u32[]{:S(2)}) copy-start(bf16[2,32,32,80]{3,2,1,0:T(8,128)(2,1)} %param.4) | copy-start | bytes 983044

commit v2 on v0

v2 whole, which is shorter than its diff:
```python
import functools

import jax
import jax.numpy as jnp
from jax import lax
from jax.experimental import pallas as pl
from jax.experimental.pallas import tpu as pltpu
from jax.sharding import PartitionSpec as P

MESH = pl.DeviceIdType.MESH
BF = jnp.bfloat16
F32 = jnp.float32


def dot(a, b, dims):
    return lax.dot_general(a, b, (dims, ((), ())), preferred_element_type=F32)


def iota(shape, dim):
    return lax.broadcasted_iota(jnp.int32, shape, dim)


def one_hot(hit):
    return jnp.where(hit, 1.0, 0.0).astype(BF)


def kernel(
    img_h, g_h, p_h, o_h, out_ref,
    img_v, g_v, o_v, o_rows, pbuf, patches, t_v,
    sp0, sp1, sp2, db0, db1, db2, ss0, ss1, ss2, rb0, rb1, rb2, hb0, hb1, hb2,
    hmat, pcat, acc, pk, pr,
    load_sem, p_send, p_recv, d_send, d_recv, rs_send, rs_recv, ag_send, ag_recv, f_send, f_recv,
):
    sp, db, ss, rb, hb = (sp0, sp1, sp2), (db0, db1, db2), (ss0, ss1, ss2), (rb0, rb1, rb2), (hb0, hb1, hb2)
    blk = lax.axis_index("blk")
    dp = lax.axis_index("dp")
    core = dp % 2
    pos = dp // 2
    x_hi = pos % 2
    z = dp // 4
    low = dp % 4
    sibling = {"blk": blk, "dp": dp + 1 - 2 * core}
    partner = {"blk": blk, "dp": dp + 2 - 4 * x_hi}
    stays = z == blk

    loads = [
        pltpu.make_async_copy(img_h, img_v, load_sem.at[0]),
        pltpu.make_async_copy(g_h, g_v, load_sem.at[1]),
        pltpu.make_async_copy(o_h, o_v, load_sem.at[2]),
        pltpu.make_async_copy(p_h, pbuf.at[low], load_sem.at[3]),
    ]
    for load in loads:
        load.start()

    barrier = pltpu.get_barrier_semaphore()

    def greet(target):
        pl.semaphore_signal(barrier, inc=1, device_id=target, device_id_type=MESH)

    for j in range(1, 16):
        greet({"blk": blk, "dp": ((pos + j) % 16) * 2 + core})
    for j in range(1, 8):
        greet({"blk": (z + 8 - j) % 8, "dp": blk * 4 + low})

    @pl.when(jnp.logical_not(stays))
    def _():
        greet({"blk": z, "dp": blk * 4 + low})

    greet(sibling)

    loads[0].wait()
    img_t = dot(one_hot(iota((80, 80), 0) == iota((80, 80), 1)), img_v[...], ((1,), (1,)))
    lane = iota((80, 2048), 1)
    col = lane & 31
    row = (lane >> 5) & 31
    zero = jnp.zeros((80, 2048), F32)
    taps = [
        jnp.where(col == 0, zero, pltpu.roll(img_t, 1, 1)),
        img_t,
        jnp.where(col == 31, zero, pltpu.roll(img_t, 2047, 1)),
    ]
    t_v[240:256, :] = jnp.zeros((16, 640), BF)

    loads[2].wait()
    r = iota((640, 640), 0)
    tail = r - 512
    main = r < 512
    r_core = jnp.where(main, r >> 8, tail >> 6)
    r_half = jnp.where(main, (r >> 4) & 1, (tail >> 5) & 1)
    r_own = jnp.where(main, (r >> 5) & 7, (tail >> 2) & 7)
    r_t = jnp.where(main, r & 15, 16 + (tail & 3))
    wanted = 80 * r_own + 40 * r_half + 20 * r_core + r_t
    o_rows[...] = dot(one_hot(iota((640, 640), 1) == wanted), o_v[...], ((1,), (0,))).astype(BF)

    def slab(m, kh):
        for kw in range(3):
            if kh == 0:
                piece = jnp.where(row == 0, zero, pltpu.roll(taps[kw], 32, 1))
            elif kh == 1:
                piece = taps[kw]
            else:
                piece = jnp.where(row == 31, zero, pltpu.roll(taps[kw], 2016, 1))
            patches[80 * kw : 80 * kw + 80, :] = piece.astype(BF)
        t_v[0:240, :] = dot(patches[...], g_v[...], ((1,), (0,))).astype(BF)
        mixed = dot(o_rows[...], t_v[...], ((1,), (1,))).astype(BF)
        sp[m][:, :, :, 0:256] = mixed[0:512].reshape(2, 16, 16, 256)
        for owner in range(2):
            for half in range(2):
                for e in range(2):
                    top = 512 + 64 * owner + 32 * half + 16 * e
                    sp2[owner, 2 * (3 * e + m) + half, :, 256:512] = mixed[top : top + 16]

    def swap(m):
        return pltpu.make_async_remote_copy(
            src_ref=sp[m].at[1 - core], dst_ref=db[m], send_sem=d_send.at[m], recv_sem=d_recv.at[m],
            device_id=sibling, device_id_type=MESH,
        )

    def scatter(m):
        copies = []
        for j in range(1, 16):
            peer = (pos + j) % 16
            copies.append(
                pltpu.make_async_remote_copy(
                    src_ref=ss[m].at[peer], dst_ref=rb[m].at[j],
                    send_sem=rs_send.at[m, j], recv_sem=rs_recv.at[m, j],
                    device_id={"blk": blk, "dp": peer * 2 + core}, device_id_type=MESH,
                )
            )
        return copies

    def gather(m):
        copies = []
        for j in range(1, 8):
            peer = (z + j) % 8
            copies.append(
                pltpu.make_async_remote_copy(
                    src_ref=hb[m].at[z], dst_ref=hb[m].at[z],
                    send_sem=ag_send.at[m, j], recv_sem=ag_recv.at[m, j],
                    device_id={"blk": blk, "dp": peer * 4 + low}, device_id_type=MESH,
                )
            )
        return copies

    def p_copy(slot, index, target):
        return pltpu.make_async_remote_copy(
            src_ref=pbuf.at[slot], dst_ref=pbuf.at[slot], send_sem=p_send.at[index], recv_sem=p_recv.at[index],
            device_id=target, device_id_type=MESH,
        )

    swaps = [swap(m) for m in range(3)]
    scatters = [scatter(m) for m in range(3)]
    gathers = [gather(m) for m in range(3)]

    def pair_sum(m):
        swaps[m].wait_recv()
        ss[m][...] = (sp[m][core].astype(F32) + db[m][...].astype(F32)).astype(BF)
        for copy in scatters[m]:
            copy.start()

    loads[1].wait()
    slab(0, 1)
    for owner in range(2):
        sp2[owner, 12:16, :, 256:512] = jnp.zeros((4, 16, 256), BF)
    pl.semaphore_wait(barrier, 23 + jnp.where(stays, 0, 1))
    swaps[0].start()
    slab(1, 0)
    swaps[1].start()
    pair_sum(0)
    slab(2, 2)
    swaps[2].start()
    pair_sum(1)
    pair_sum(2)

    loads[3].wait()
    theirs = (low + 2) % 4
    p_out = p_copy(low, 0, partner)
    p_side = p_copy(low, 1, sibling)
    p_fwd = p_copy(theirs, 2, sibling)
    p_out.start()
    p_side.start()

    for m in range(3):
        for copy in scatters[m]:
            copy.wait_recv()
        total = ss[m][pos].astype(F32)
        for j in range(1, 16):
            total = total + rb[m][j].astype(F32)
        hb[m][z] = total.astype(BF)
        for copy in gathers[m]:
            copy.start()
        if m == 0:
            p_out.wait_recv()
            p_fwd.start()

    p_side.wait_recv()
    p_fwd.wait_recv()
    c = iota((768, 720), 0)
    part = c >> 8
    within = c & 255
    kw = (within * 52429) >> 22
    kh = jnp.where(part == 0, 1, jnp.where(part == 1, 0, 2))
    source = jnp.where(within < 240, (within - 80 * kw) * 9 + 3 * kh + kw, -1)
    order = one_hot(iota((768, 720), 1) == source)
    stacked = jnp.concatenate([dot(pbuf[s], order, ((1,), (1,))) for s in range(4)], axis=0)
    pcat[0:720, :] = stacked.astype(BF)
    pcat[720:768, :] = jnp.zeros((48, 768), BF)

    for m in range(3):
        for copy in gathers[m]:
            copy.wait_recv()
        for k in range(8):
            hmat[16 * k : 16 * k + 16, 256 * m : 256 * m + 256] = hb[m][k, :, 0:256]
    for m in range(3):
        for e in range(2):
            hmat[128 + 16 * e : 144 + 16 * e, 256 * m : 256 * m + 256] = hb2[3 * e + m, :, 256:512]
    acc[...] = dot(hmat[...], pcat[...], ((1,), (1,)))

    for k in range(8):
        pk[k, :, 0:768] = acc[16 * k : 16 * k + 16, :].astype(BF)
        tail = acc[128 + 4 * k : 132 + 4 * k, :]
        pieces = [tail[:, 0:256], tail[:, 256:512], tail[:, 512:768], jnp.zeros((4, 256), F32)]
        pk[k, :, 768:1024] = jnp.concatenate(pieces, axis=0).astype(BF)
    finals = []
    for j in range(8):
        peer = (blk + j) % 8
        finals.append(
            pltpu.make_async_remote_copy(
                src_ref=pk.at[peer], dst_ref=pr.at[j], send_sem=f_send.at[j], recv_sem=f_recv.at[j],
                device_id={"blk": z, "dp": peer * 4 + low}, device_id_type=MESH,
            )
        )
    for copy in finals[1:]:
        copy.start()

    @pl.when(jnp.logical_not(stays))
    def _():
        finals[0].start()
        finals[0].wait_recv()

    @pl.when(stays)
    def _():
        pr[0] = pk[blk]

    total = pr[0].astype(F32)
    for j in range(1, 8):
        finals[j].wait_recv()
        total = total + pr[j].astype(F32)
    out_ref[0:16, :] = total[:, 0:720]
    out_ref[16:20, 0:256] = total[0:4, 768:1024]
    out_ref[16:20, 256:512] = total[4:8, 768:1024]
    out_ref[16:20, 512:720] = total[8:12, 768:976]

    for copy in swaps + [p_out, p_side, p_fwd] + finals[1:]:
        copy.wait_send()
    for m in range(3):
        for copy in scatters[m] + gathers[m]:
            copy.wait_send()

    @pl.when(jnp.logical_not(stays))
    def _():
        finals[0].wait_send()


def on_device(images, out_grads, patch_inverse, output_inverse):
    dma = pltpu.SemaphoreType.DMA
    return pl.pallas_call(
        kernel,
        out_shape=jax.ShapeDtypeStruct((20, 720), F32),
        in_specs=[pl.BlockSpec(memory_space=pl.ANY)] * 4,
        out_specs=pl.BlockSpec(memory_space=pltpu.VMEM),
        scratch_shapes=[
            pltpu.VMEM((2048, 80), BF),
            pltpu.VMEM((2048, 640), BF),
            pltpu.VMEM((640, 640), BF),
            pltpu.VMEM((640, 640), BF),
            pltpu.VMEM((4, 180, 720), BF),
            pltpu.VMEM((240, 2048), BF),
            pltpu.VMEM((256, 640), BF),
            pltpu.VMEM((2, 16, 16, 256), BF),
            pltpu.VMEM((2, 16, 16, 256), BF),
            pltpu.VMEM((2, 16, 16, 512), BF),
            pltpu.VMEM((16, 16, 256), BF),
            pltpu.VMEM((16, 16, 256), BF),
            pltpu.VMEM((16, 16, 512), BF),
            pltpu.VMEM((16, 16, 256), BF),
            pltpu.VMEM((16, 16, 256), BF),
            pltpu.VMEM((16, 16, 512), BF),
            pltpu.VMEM((16, 16, 256), BF),
            pltpu.VMEM((16, 16, 256), BF),
            pltpu.VMEM((16, 16, 512), BF),
            pltpu.VMEM((8, 16, 256), BF),
            pltpu.VMEM((8, 16, 256), BF),
            pltpu.VMEM((8, 16, 512), BF),
            pltpu.VMEM((160, 768), BF),
            pltpu.VMEM((768, 768), BF),
            pltpu.VMEM((160, 768), F32),
            pltpu.VMEM((8, 16, 1024), BF),
            pltpu.VMEM((8, 16, 1024), BF),
            dma((4,)),
            dma((3,)), dma((3,)),
            dma((3,)), dma((3,)),
            dma((3, 16)), dma((3, 16)),
            dma((3, 8)), dma((3, 8)),
            dma((8,)), dma((8,)),
        ],
        compiler_params=pltpu.CompilerParams(
            collective_id=0, has_side_effects=True, vmem_limit_bytes=60 * 1024 * 1024
        ),
        cost_estimate=pl.CostEstimate(flops=3 * 10**9, bytes_accessed=5 * 10**6, transcendentals=0),
    )(
        images.reshape(2048, 80),
        out_grads.reshape(2048, 640),
        patch_inverse.T,
        output_inverse,
    )


def solution(mesh):
    placed = (P("dp", None, None, "blk"), P("dp", None, None, None), P("blk", "dp"), P())
    return jax.shard_map(
        on_device, mesh=mesh, in_specs=placed, out_specs=P("dp", "blk"), check_vma=False
    )
```

time: 367 us -> 48.9 us (0.13)
  waiting for transfers between devices: 199 us -> 0 us
  local copies, waits for them, and re-layouts: 64.2 us -> 1.52 us
  blocking collectives: 58.1 us -> 0 us
  Pallas kernels: 0 us -> 47.3 us
  matrix products: 19.7 us -> 0 us
  between operations: 13.4 us -> 0.01 us
  other arithmetic: 9.98 us -> 0 us
    all_gather x2 -> x0, waiting for transfers between devices: 199 us -> none  [the longest x1 138 us: on_device(): lax.all_gather(grad_slab, 'blk', axis=1, tiled=True)]
    all_to_all x1 -> x0, blocking collectives: 58.1 us -> none  [on_device(): lax.all_to_all(mixed[None], 'dp', split_axis=1, concat_axis=0, tiled=True)]
    pallas_call x0 -> x1, Pallas kernels: none -> 47.3 us  [on_device(): pl.pallas_call(kernel, out_shape=jax.ShapeDtypeStruct((20, 720), F32), in...]
    unnamed x15 -> x1, local copies, waits for them, and re-layouts: 25.2 us -> 1.52 us
    dot_general x3 -> x0, matrix products: 19.7 us -> none  [the longest x1 10.7 us: on_device(): lax.dot_general(lax.all_gather(grad_slab, 'blk', axis=1, tiled=True), inv...]
    reshape x1 -> x0, local copies, waits for them, and re-layouts: 16.4 us -> none  [patch_rows(): return stacked.reshape(-1, images.shape[3] * 9)]
    another operation x2 -> x0, local copies, waits for them, and re-layouts: 14.7 us -> none  [patch_rows(): stacked = jnp.stack(shifted, axis=-1)]
    all_to_all x1 -> x0, other arithmetic: 7.55 us -> none  [on_device(): lax.all_to_all(mixed[None], 'dp', split_axis=1, concat_axis=0, tiled=True)]
  transfers between devices with their start and end apart: 2 -> 0, of which waited for: 2 -> 0; matrix products, arithmetic and copies ran while one was open for 17% -> 0% of each run, Pallas kernels for 0% -> 0%
where the time goes in v2:
time: 48.9 us; the launch traced here: 48.8 us
  Pallas kernels  47.3 us (97%)
  local copies, waits for them, and re-layouts  1.52 us (3%)
    pallas_call x1, Pallas kernels, on_device(): pl.pallas_call(kernel, out_shape=jax.ShapeDtypeStruct((20, 720), F32), in...  47.3 us
    unnamed x1, local copies, waits for them, and re-layouts  1.52 us

profile of v2, /device:TPU:2, one launch (start us, length us, event | category | flops | bytes accessed | tf_op | source)
XLA Modules:
  0.0 48.8 jit_solution(11633177915524531808)
XLA Ops:
  0.0 47.3 %shard_map.46 = f32[20,720]{1,0:T(8,128)} custom-call(bf16[2048,80]{1,0:T(8,128)(2,1)} %bitcast.4, bf16[2048,640]{1,0:T(8,128)(2,1)} %bitcast.3, bf16[180,720]{1,0:T(8,128)(2,1)} %bitcast.5, bf16[640,640]{1,0:T(8,128)(2,1)} %o_h.1), custom_call_target="tpu_custom_call" | custom-call | flops 3000000000 | bytes 5000000 | tf_op jit(solution)/shard_map/pallas_call | solution.py:267
  47.3 1.5 %copy.6 = f32[20,720]{1,0:T(8,128)} copy(f32[20,720]{1,0:T(8,128)} %shard_map.46) | data formatting | bytes 115200

commit v3 on v2

v3 whole, which is shorter than its diff:
```python
import functools

import jax
import jax.numpy as jnp
from jax import lax
from jax.experimental import pallas as pl
from jax.experimental.pallas import tpu as pltpu
from jax.sharding import PartitionSpec as P

MESH = pl.DeviceIdType.MESH
BF = jnp.bfloat16
F32 = jnp.float32


def dot(a, b, dims):
    return lax.dot_general(a, b, (dims, ((), ())), preferred_element_type=F32)


def iota(shape, dim):
    return lax.broadcasted_iota(jnp.int32, shape, dim)


def one_hot(hit):
    return jnp.where(hit, 1.0, 0.0).astype(BF)


def kernel(
    img_h, g_h, p_h, o_h, out_ref,
    img_v, g_v, o_v, o_rows, pbuf, patches, t_v,
    sp, db, ss, xb, su, rb, hb,
    hmat, pcat, acc, main_out, main_in, tail_out, tail_in,
    load_sem, p_send, p_recv, d_send, d_recv, x_send, x_recv, rs_send, rs_recv, ag_send, ag_recv,
    m_send, m_recv, t_send, t_recv,
):
    blk = lax.axis_index("blk")
    dp = lax.axis_index("dp")
    core = dp % 2
    x_hi = (dp // 2) % 2
    z = dp // 4
    low = dp % 4
    sibling = {"blk": blk, "dp": dp + 1 - 2 * core}
    partner = {"blk": blk, "dp": dp + 2 - 4 * x_hi}
    stays = z == blk

    loads = [
        pltpu.make_async_copy(img_h, img_v, load_sem.at[0]),
        pltpu.make_async_copy(g_h, g_v, load_sem.at[1]),
        pltpu.make_async_copy(o_h, o_v, load_sem.at[2]),
        pltpu.make_async_copy(p_h, pbuf.at[low], load_sem.at[3]),
    ]
    for load in loads:
        load.start()

    barrier = pltpu.get_barrier_semaphore()

    def greet(target):
        pl.semaphore_signal(barrier, inc=1, device_id=target, device_id_type=MESH)

    for j in range(1, 8):
        greet({"blk": (z + 8 - j) % 8, "dp": blk * 4 + low})

    @pl.when(jnp.logical_not(stays))
    def _():
        greet({"blk": z, "dp": blk * 4 + low})

    for j in range(1, 8):
        greet({"blk": blk, "dp": ((z + j) % 8) * 4 + low})
    greet(partner)
    greet(sibling)

    loads[0].wait()
    img_t = dot(one_hot(iota((80, 80), 0) == iota((80, 80), 1)), img_v[...], ((1,), (1,)))
    lane = iota((80, 2048), 1)
    col = lane & 31
    row = (lane >> 5) & 31
    zero = jnp.zeros((80, 2048), F32)
    taps = [
        jnp.where(col == 0, zero, pltpu.roll(img_t, 1, 1)),
        img_t,
        jnp.where(col == 31, zero, pltpu.roll(img_t, 2047, 1)),
    ]
    t_v[240:256, :] = jnp.zeros((16, 640), BF)

    loads[2].wait()
    r = iota((640, 1), 0)
    rest = r - 512
    main = r < 512
    r_core = jnp.where(main, r >> 8, rest >> 6)
    r_half = jnp.where(main, (r >> 7) & 1, (rest >> 5) & 1)
    r_own = jnp.where(main, (r >> 4) & 7, (rest >> 2) & 7)
    r_t = jnp.where(main, r & 15, 16 + (rest & 3))
    wanted = 80 * r_own + 40 * r_half + 20 * r_core + r_t
    o_rows[...] = dot(one_hot(iota((640, 640), 1) == wanted), o_v[...], ((1,), (0,))).astype(BF)

    def slab(m, kh):
        for kw in range(3):
            if kh == 0:
                piece = jnp.where(row == 0, zero, pltpu.roll(taps[kw], 32, 1))
            elif kh == 1:
                piece = taps[kw]
            else:
                piece = jnp.where(row == 31, zero, pltpu.roll(taps[kw], 2016, 1))
            patches[80 * kw : 80 * kw + 80, :] = piece.astype(BF)
        t_v[0:240, :] = dot(patches[...], g_v[...], ((1,), (0,))).astype(BF)
        mixed = dot(o_rows[...], t_v[...], ((1,), (1,))).astype(BF)
        sp[m] = mixed[0:512].reshape(2, 2, 8, 16, 256)
        for owner in range(2):
            for half in range(2):
                for e in range(2):
                    top = 512 + 64 * owner + 32 * half + 16 * e
                    sp[3, owner, half, 3 * e + m] = mixed[top : top + 16]

    def remote(src, dst, send, recv, target):
        return pltpu.make_async_remote_copy(
            src_ref=src, dst_ref=dst, send_sem=send, recv_sem=recv, device_id=target, device_id_type=MESH
        )

    swaps = [remote(sp.at[q, 1 - core], db.at[q], d_send.at[q], d_recv.at[q], sibling) for q in range(4)]
    sides = [remote(ss.at[q, 1 - x_hi], xb.at[q], x_send.at[q], x_recv.at[q], partner) for q in range(4)]
    scatters = [[] for q in range(4)]
    gathers = [[] for q in range(4)]
    for q in range(4):
        for j in (4, 3, 5, 2, 6, 1, 7):
            peer = (z + j) % 8
            target = {"blk": blk, "dp": peer * 4 + low}
            scatters[q].append(
                remote(su.at[q, peer], rb.at[q, j], rs_send.at[q, j], rs_recv.at[q, j], target)
            )
            gathers[q].append(
                remote(hb.at[q, z], hb.at[q, z], ag_send.at[q, j], ag_recv.at[q, j], target)
            )
    theirs = (low + 2) % 4
    p_out = remote(pbuf.at[low], pbuf.at[low], p_send.at[0], p_recv.at[0], partner)
    p_side = remote(pbuf.at[low], pbuf.at[low], p_send.at[1], p_recv.at[1], sibling)
    p_fwd = remote(pbuf.at[theirs], pbuf.at[theirs], p_send.at[2], p_recv.at[2], sibling)
    mains = []
    tails = []
    for j in range(8):
        peer = (blk + j) % 8
        target = {"blk": z, "dp": peer * 4 + low}
        mains.append(remote(main_out.at[peer], main_in.at[j], m_send.at[j], m_recv.at[j], target))
        tails.append(remote(tail_out.at[peer], tail_in.at[j], t_send.at[j], t_recv.at[j], target))

    def pair_sum(q):
        swaps[q].wait_recv()
        ss[q] = (sp[q, core].astype(F32) + db[q].astype(F32)).astype(BF)
        sides[q].start()

    loads[1].wait()
    slab(0, 1)
    pl.semaphore_wait(barrier, 16 + jnp.where(stays, 0, 1))
    swaps[0].start()
    for owner in range(2):
        for half in range(2):
            sp[3, owner, half, 6:8] = jnp.zeros((2, 16, 256), BF)
    slab(1, 0)
    swaps[1].start()
    pair_sum(0)
    slab(2, 2)
    swaps[2].start()
    swaps[3].start()
    pair_sum(1)
    pair_sum(2)
    pair_sum(3)

    loads[3].wait()
    p_out.start()
    p_side.start()

    for q in range(4):
        sides[q].wait_recv()
        su[q] = (ss[q, x_hi].astype(F32) + xb[q].astype(F32)).astype(BF)
        for copy in scatters[q]:
            copy.start()

    for q in range(4):
        total = su[q, z].astype(F32)
        for copy in scatters[q]:
            copy.wait_recv()
        for j in range(1, 8):
            total = total + rb[q, j].astype(F32)
        hb[q, z] = total.astype(BF)
        for copy in gathers[q]:
            copy.start()
        if q == 1:
            p_out.wait_recv()
            p_fwd.start()

    p_side.wait_recv()
    p_fwd.wait_recv()
    c = iota((768, 1), 0)
    part = c >> 8
    within = c & 255
    kw = (within * 52429) >> 22
    kh = jnp.where(part == 0, 1, jnp.where(part == 1, 0, 2))
    source = jnp.where(within < 240, (within - 80 * kw) * 9 + 3 * kh + kw, -1)
    order = one_hot(iota((768, 720), 1) == source)
    stacked = jnp.concatenate([dot(pbuf[s], order, ((1,), (1,))) for s in range(4)], axis=0)
    pcat[0:720, :] = stacked.astype(BF)
    pcat[720:768, :] = jnp.zeros((48, 768), BF)

    for q in range(3):
        for copy in gathers[q]:
            copy.wait_recv()
        hmat[0:128, 256 * q : 256 * q + 256] = hb[q].reshape(128, 256)
    rows = dot(hmat[0:128, :], pcat[...], ((1,), (1,)))

    main_out[...] = rows.astype(BF).reshape(8, 16, 768)
    for copy in mains[1:]:
        copy.start()

    @pl.when(jnp.logical_not(stays))
    def _():
        mains[0].start()

    for copy in gathers[3]:
        copy.wait_recv()
    for m in range(3):
        for e in range(2):
            hmat[128 + 16 * e : 144 + 16 * e, 256 * m : 256 * m + 256] = hb[3, 3 * e + m]
    acc[...] = dot(hmat[128:160, :], pcat[...], ((1,), (1,)))
    for k in range(8):
        tail = acc[4 * k : 4 * k + 4, :]
        pieces = [tail[:, 0:256], tail[:, 256:512], tail[:, 512:768], jnp.zeros((4, 256), F32)]
        tail_out[k] = jnp.concatenate(pieces, axis=0).astype(BF)
    for copy in tails[1:]:
        copy.start()

    @pl.when(jnp.logical_not(stays))
    def _():
        tails[0].start()
        mains[0].wait_recv()

    @pl.when(stays)
    def _():
        main_in[0] = main_out[blk]
        tail_in[0] = tail_out[blk]

    total = main_in[0].astype(F32)
    for j in range(1, 8):
        mains[j].wait_recv()
        total = total + main_in[j].astype(F32)
    out_ref[0:16, :] = total[:, 0:720]

    @pl.when(jnp.logical_not(stays))
    def _():
        tails[0].wait_recv()

    total = tail_in[0].astype(F32)
    for j in range(1, 8):
        tails[j].wait_recv()
        total = total + tail_in[j].astype(F32)
    out_ref[16:20, 0:256] = total[0:4, :]
    out_ref[16:20, 256:512] = total[4:8, :]
    out_ref[16:20, 512:720] = total[8:12, 0:208]

    for copy in swaps + sides + [p_out, p_side, p_fwd] + mains[1:] + tails[1:]:
        copy.wait_send()
    for q in range(4):
        for copy in scatters[q] + gathers[q]:
            copy.wait_send()

    @pl.when(jnp.logical_not(stays))
    def _():
        mains[0].wait_send()
        tails[0].wait_send()


def on_device(images, out_grads, patch_inverse, output_inverse):
    dma = pltpu.SemaphoreType.DMA
    return pl.pallas_call(
        kernel,
        out_shape=jax.ShapeDtypeStruct((20, 720), F32),
        in_specs=[pl.BlockSpec(memory_space=pl.ANY)] * 4,
        out_specs=pl.BlockSpec(memory_space=pltpu.VMEM),
        scratch_shapes=[
            pltpu.VMEM((2048, 80), BF),
            pltpu.VMEM((2048, 640), BF),
            pltpu.VMEM((640, 640), BF),
            pltpu.VMEM((640, 640), BF),
            pltpu.VMEM((4, 180, 720), BF),
            pltpu.VMEM((240, 2048), BF),
            pltpu.VMEM((256, 640), BF),
            pltpu.VMEM((4, 2, 2, 8, 16, 256), BF),
            pltpu.VMEM((4, 2, 8, 16, 256), BF),
            pltpu.VMEM((4, 2, 8, 16, 256), BF),
            pltpu.VMEM((4, 8, 16, 256), BF),
            pltpu.VMEM((4, 8, 16, 256), BF),
            pltpu.VMEM((4, 8, 16, 256), BF),
            pltpu.VMEM((4, 8, 16, 256), BF),
            pltpu.VMEM((160, 768), BF),
            pltpu.VMEM((768, 768), BF),
            pltpu.VMEM((32, 768), F32),
            pltpu.VMEM((8, 16, 768), BF),
            pltpu.VMEM((8, 16, 768), BF),
            pltpu.VMEM((8, 16, 256), BF),
            pltpu.VMEM((8, 16, 256), BF),
            dma((4,)),
            dma((3,)), dma((3,)),
            dma((4,)), dma((4,)),
            dma((4,)), dma((4,)),
            dma((4, 8)), dma((4, 8)),
            dma((4, 8)), dma((4, 8)),
            dma((8,)), dma((8,)),
            dma((8,)), dma((8,)),
        ],
        compiler_params=pltpu.CompilerParams(
            collective_id=0, has_side_effects=True, vmem_limit_bytes=60 * 1024 * 1024
        ),
        cost_estimate=pl.CostEstimate(flops=3 * 10**9, bytes_accessed=5 * 10**6, transcendentals=0),
    )(
        images.reshape(2048, 80),
        out_grads.reshape(2048, 640),
        patch_inverse.T,
        output_inverse,
    )


def solution(mesh):
    placed = (P("dp", None, None, "blk"), P("dp", None, None, None), P("blk", "dp"), P())
    return jax.shard_map(
        on_device, mesh=mesh, in_specs=placed, out_specs=P("dp", "blk"), check_vma=False
    )
```

time: 48.9 us -> 44.7 us (0.914)
  Pallas kernels: 47.3 us -> 43 us
    pallas_call x1, Pallas kernels: 47.3 us -> 43 us  [on_device(): pl.pallas_call(kernel, out_shape=jax.ShapeDtypeStruct((20, 720), F32), in...]
where the time goes in v3:
time: 44.7 us; the launch traced here: 44.6 us
  Pallas kernels  43 us (96%)
  local copies, waits for them, and re-layouts  1.52 us (3%)
    pallas_call x1, Pallas kernels, on_device(): pl.pallas_call(kernel, out_shape=jax.ShapeDtypeStruct((20, 720), F32), in...  43 us
    unnamed x1, local copies, waits for them, and re-layouts  1.52 us

profile of v3, /device:TPU:2, one launch (start us, length us, event | category | flops | bytes accessed | tf_op | source)
XLA Modules:
  0.0 44.6 jit_solution(18174804024742394021)
XLA Ops:
  0.0 43.0 %shard_map.46 = f32[20,720]{1,0:T(8,128)} custom-call(bf16[2048,80]{1,0:T(8,128)(2,1)} %bitcast.4, bf16[2048,640]{1,0:T(8,128)(2,1)} %bitcast.3, bf16[180,720]{1,0:T(8,128)(2,1)} %bitcast.5, bf16[640,640]{1,0:T(8,128)(2,1)} %o_h.1), custom_call_target="tpu_custom_call" | custom-call | flops 3000000000 | bytes 5000000 | tf_op jit(solution)/shard_map/pallas_call | solution.py:271
  43.0 1.5 %copy.6 = f32[20,720]{1,0:T(8,128)} copy(f32[20,720]{1,0:T(8,128)} %shard_map.46) | data formatting | bytes 115200

commit v4 on v3

--- a/solution.py
+++ b/solution.py
@@ -89,10 +89,10 @@
     r_half = jnp.where(main, (r >> 7) & 1, (rest >> 5) & 1)
     r_own = jnp.where(main, (r >> 4) & 7, (rest >> 2) & 7)
     r_t = jnp.where(main, r & 15, 16 + (rest & 3))
-    wanted = 80 * r_own + 40 * r_half + 20 * r_core + r_t
+    wanted = 80 * ((r_own + 4) & 7) + 40 * r_half + 20 * r_core + r_t
     o_rows[...] = dot(one_hot(iota((640, 640), 1) == wanted), o_v[...], ((1,), (0,))).astype(BF)
 
-    def slab(m, kh):
+    def slab(m, kh, between=None):
         for kw in range(3):
             if kh == 0:
                 piece = jnp.where(row == 0, zero, pltpu.roll(taps[kw], 32, 1))
@@ -102,6 +102,8 @@
                 piece = jnp.where(row == 31, zero, pltpu.roll(taps[kw], 2016, 1))
             patches[80 * kw : 80 * kw + 80, :] = piece.astype(BF)
         t_v[0:240, :] = dot(patches[...], g_v[...], ((1,), (0,))).astype(BF)
+        if between is not None:
+            pair_sum(between)
         mixed = dot(o_rows[...], t_v[...], ((1,), (1,))).astype(BF)
         sp[m] = mixed[0:512].reshape(2, 2, 8, 16, 256)
         for owner in range(2):
@@ -116,11 +118,17 @@
         )
 
     swaps = [remote(sp.at[q, 1 - core], db.at[q], d_send.at[q], d_recv.at[q], sibling) for q in range(4)]
-    sides = [remote(ss.at[q, 1 - x_hi], xb.at[q], x_send.at[q], x_recv.at[q], partner) for q in range(4)]
+    sides = [
+        remote(
+            ss.at[q, 1 - x_hi, pl.ds(0, n)], xb.at[q, pl.ds(0, n)], x_send.at[q], x_recv.at[q], partner
+        )
+        for q, n in enumerate((8, 8, 8, 6))
+    ]
+    far_first = (4, 3, 5, 2, 6, 1, 7)
     scatters = [[] for q in range(4)]
     gathers = [[] for q in range(4)]
     for q in range(4):
-        for j in (4, 3, 5, 2, 6, 1, 7):
+        for j in far_first:
             peer = (z + j) % 8
             target = {"blk": blk, "dp": peer * 4 + low}
             scatters[q].append(
@@ -133,14 +141,6 @@
     p_out = remote(pbuf.at[low], pbuf.at[low], p_send.at[0], p_recv.at[0], partner)
     p_side = remote(pbuf.at[low], pbuf.at[low], p_send.at[1], p_recv.at[1], sibling)
     p_fwd = remote(pbuf.at[theirs], pbuf.at[theirs], p_send.at[2], p_recv.at[2], sibling)
-    mains = []
-    tails = []
-    for j in range(8):
-        peer = (blk + j) % 8
-        target = {"blk": z, "dp": peer * 4 + low}
-        mains.append(remote(main_out.at[peer], main_in.at[j], m_send.at[j], m_recv.at[j], target))
-        tails.append(remote(tail_out.at[peer], tail_in.at[j], t_send.at[j], t_recv.at[j], target))
-
     def pair_sum(q):
         swaps[q].wait_recv()
         ss[q] = (sp[q, core].astype(F32) + db[q].astype(F32)).astype(BF)
@@ -153,13 +153,13 @@
     for owner in range(2):
         for half in range(2):
             sp[3, owner, half, 6:8] = jnp.zeros((2, 16, 256), BF)
+    xb[3, 6:8] = jnp.zeros((2, 16, 256), BF)
     slab(1, 0)
     swaps[1].start()
     pair_sum(0)
-    slab(2, 2)
+    slab(2, 2, 1)
     swaps[2].start()
     swaps[3].start()
-    pair_sum(1)
     pair_sum(2)
     pair_sum(3)
 
@@ -182,9 +182,8 @@
         hb[q, z] = total.astype(BF)
         for copy in gathers[q]:
             copy.start()
-        if q == 1:
-            p_out.wait_recv()
-            p_fwd.start()
+    p_out.wait_recv()
+    p_fwd.start()
 
     p_side.wait_recv()
     p_fwd.wait_recv()
@@ -199,62 +198,83 @@
     pcat[0:720, :] = stacked.astype(BF)
     pcat[720:768, :] = jnp.zeros((48, 768), BF)
 
-    for q in range(3):
-        for copy in gathers[q]:
-            copy.wait_recv()
-        hmat[0:128, 256 * q : 256 * q + 256] = hb[q].reshape(128, 256)
-    rows = dot(hmat[0:128, :], pcat[...], ((1,), (1,)))
-
-    main_out[...] = rows.astype(BF).reshape(8, 16, 768)
-    for copy in mains[1:]:
-        copy.start()
-
-    @pl.when(jnp.logical_not(stays))
-    def _():
-        mains[0].start()
+    def to_plane(outgoing, incoming, send, recv, j):
+        plane = (z + 12 - j) % 8
+        return remote(
+            outgoing.at[plane], incoming.at[blk], send.at[j], recv.at[blk], {"blk": z, "dp": plane * 4 + low}
+        )
+
+    def from_column(outgoing, incoming, send, recv, b):
+        return remote(outgoing.at[b], incoming.at[b], send.at[0], recv.at[b], {"blk": b, "dp": blk * 4 + low})
+
+    mains = [to_plane(main_out, main_in, m_send, m_recv, j) for j in range(8)]
+    tails = [to_plane(tail_out, tail_in, t_send, t_recv, j) for j in range(8)]
+
+    def send_rows(group, extra=0):
+        for q in range(3):
+            for copy, j in zip(gathers[q], far_first):
+                if j in group:
+                    copy.wait_recv()
+        for i, j in enumerate(group):
+            for q in range(3):
+                hmat[16 * i : 16 * i + 16, 256 * q : 256 * q + 256] = hb[q, (z + 8 - j) % 8]
+        n = 16 * len(group)
+        product = dot(hmat[0 : n + extra, :], pcat[...], ((1,), (1,)))
+        rows = product[0:n].astype(BF)
+        for i, j in enumerate(group):
+            main_out[(z + 12 - j) % 8] = rows[16 * i : 16 * i + 16, :]
+        for j in group:
+            if j == 4:
+                @pl.when(jnp.logical_not(stays))
+                def _():
+                    mains[4].start()
+            else:
+                mains[j].start()
+        return product[n:]
+
+    send_rows((0, 1, 7, 2, 6))
 
     for copy in gathers[3]:
         copy.wait_recv()
     for m in range(3):
         for e in range(2):
-            hmat[128 + 16 * e : 144 + 16 * e, 256 * m : 256 * m + 256] = hb[3, 3 * e + m]
-    acc[...] = dot(hmat[128:160, :], pcat[...], ((1,), (1,)))
+            hmat[48 + 16 * e : 64 + 16 * e, 256 * m : 256 * m + 256] = hb[3, 3 * e + m]
+    acc[...] = send_rows((3, 5, 4), 32)
     for k in range(8):
         tail = acc[4 * k : 4 * k + 4, :]
         pieces = [tail[:, 0:256], tail[:, 256:512], tail[:, 512:768], jnp.zeros((4, 256), F32)]
-        tail_out[k] = jnp.concatenate(pieces, axis=0).astype(BF)
-    for copy in tails[1:]:
-        copy.start()
+        tail_out[(k + 4) % 8] = jnp.concatenate(pieces, axis=0).astype(BF)
+    for j in (0, 1, 7, 2, 6, 3, 5):
+        tails[j].start()
 
     @pl.when(jnp.logical_not(stays))
     def _():
-        tails[0].start()
-        mains[0].wait_recv()
+        tails[4].start()
+
 
     @pl.when(stays)
     def _():
-        main_in[0] = main_out[blk]
-        tail_in[0] = tail_out[blk]
-
-    total = main_in[0].astype(F32)
-    for j in range(1, 8):
-        mains[j].wait_recv()
-        total = total + main_in[j].astype(F32)
+        main_in[blk] = main_out[z]
+        tail_in[blk] = tail_out[z]
+
+    def collect(outgoing, incoming, send, recv):
+        total = jnp.zeros(incoming.shape[1:], F32)
+        for b in range(8):
+            @pl.when(jnp.logical_not(jnp.logical_and(stays, blk == b)))
+            def _():
+                from_column(outgoing, incoming, send, recv, b).wait_recv()
+
+            total = total + incoming[b].astype(F32)
+        return total
+
+    total = collect(main_out, main_in, m_send, m_recv)
     out_ref[0:16, :] = total[:, 0:720]
-
-    @pl.when(jnp.logical_not(stays))
-    def _():
-        tails[0].wait_recv()
-
-    total = tail_in[0].astype(F32)
-    for j in range(1, 8):
-        tails[j].wait_recv()
-        total = total + tail_in[j].astype(F32)
+    total = collect(tail_out, tail_in, t_send, t_recv)
     out_ref[16:20, 0:256] = total[0:4, :]
     out_ref[16:20, 256:512] = total[4:8, :]
     out_ref[16:20, 512:720] = total[8:12, 0:208]
 
-    for copy in swaps + sides + [p_out, p_side, p_fwd] + mains[1:] + tails[1:]:
+    for copy in swaps + sides + [p_out, p_side, p_fwd] + mains[:4] + mains[5:] + tails[:4] + tails[5:]:
         copy.wait_send()
     for q in range(4):
         for copy in scatters[q] + gathers[q]:
@@ -262,8 +282,8 @@
 
     @pl.when(jnp.logical_not(stays))
     def _():
-        mains[0].wait_send()
-        tails[0].wait_send()
+        mains[4].wait_send()
+        tails[4].wait_send()
 
 
 def on_device(images, out_grads, patch_inverse, output_inverse):

time: 44.7 us -> 43.5 us (0.973)
  Pallas kernels: 43 us -> 41.9 us
    pallas_call x1, Pallas kernels: 43 us -> 41.9 us  [on_device(): pl.pallas_call(kernel, out_shape=jax.ShapeDtypeStruct((20, 720), F32), in...]
where the time goes in v4:
time: 43.5 us; the launch traced here: 43.4 us
  Pallas kernels  41.9 us (96%)
  local copies, waits for them, and re-layouts  1.52 us (3%)
    pallas_call x1, Pallas kernels, on_device(): pl.pallas_call(kernel, out_shape=jax.ShapeDtypeStruct((20, 720), F32), in...  41.9 us
    unnamed x1, local copies, waits for them, and re-layouts  1.52 us

profile of v4, /device:TPU:2, one launch (start us, length us, event | category | flops | bytes accessed | tf_op | source)
XLA Modules:
  0.0 43.4 jit_solution(15165022470855510308)
XLA Ops:
  0.0 41.9 %shard_map.46 = f32[20,720]{1,0:T(8,128)} custom-call(bf16[2048,80]{1,0:T(8,128)(2,1)} %bitcast.4, bf16[2048,640]{1,0:T(8,128)(2,1)} %bitcast.3, bf16[180,720]{1,0:T(8,128)(2,1)} %bitcast.5, bf16[640,640]{1,0:T(8,128)(2,1)} %o_h.1), custom_call_target="tpu_custom_call" | custom-call | flops 3000000000 | bytes 5000000 | tf_op jit(solution)/shard_map/pallas_call | solution.py:291
  41.9 1.5 %copy.6 = f32[20,720]{1,0:T(8,128)} copy(f32[20,720]{1,0:T(8,128)} %shard_map.46) | data formatting | bytes 115200

commit v5 on v4

--- a/solution.py
+++ b/solution.py
@@ -10,6 +10,8 @@
 MESH = pl.DeviceIdType.MESH
 BF = jnp.bfloat16
 F32 = jnp.float32
+LATE = (2,)
+STEPS = (('cross', 2), ('give', 0), ('give', 1), ('give', 2), ('give', 3))
 
 
 def dot(a, b, dims):
@@ -27,7 +29,7 @@
 def kernel(
     img_h, g_h, p_h, o_h, out_ref,
     img_v, g_v, o_v, o_rows, pbuf, patches, t_v,
-    sp, db, ss, xb, su, rb, hb,
+    sp, db, ss, xb, su, rb, rz, zf, zb, zx, hb,
     hmat, pcat, acc, main_out, main_in, tail_out, tail_in,
     load_sem, p_send, p_recv, d_send, d_recv, x_send, x_recv, rs_send, rs_recv, ag_send, ag_recv,
     m_send, m_recv, t_send, t_recv,
@@ -118,12 +120,16 @@
         )
 
     swaps = [remote(sp.at[q, 1 - core], db.at[q], d_send.at[q], d_recv.at[q], sibling) for q in range(4)]
-    sides = [
-        remote(
+    sides = {
+        q: remote(
             ss.at[q, 1 - x_hi, pl.ds(0, n)], xb.at[q, pl.ds(0, n)], x_send.at[q], x_recv.at[q], partner
         )
         for q, n in enumerate((8, 8, 8, 6))
-    ]
+        if q not in LATE
+    }
+    late_sides = {
+        q: remote(zb.at[i, 1 - x_hi], zx.at[i], x_send.at[q], x_recv.at[q], partner) for i, q in enumerate(LATE)
+    }
     far_first = (4, 3, 5, 2, 6, 1, 7)
     scatters = [[] for q in range(4)]
     gathers = [[] for q in range(4)]
@@ -131,9 +137,9 @@
         for j in far_first:
             peer = (z + j) % 8
             target = {"blk": blk, "dp": peer * 4 + low}
-            scatters[q].append(
-                remote(su.at[q, peer], rb.at[q, j], rs_send.at[q, j], rs_recv.at[q, j], target)
-            )
+            source = ss.at[q, :, peer] if q in LATE else su.at[q, peer]
+            landing = rz.at[LATE.index(q), j] if q in LATE else rb.at[q, j]
+            scatters[q].append(remote(source, landing, rs_send.at[q, j], rs_recv.at[q, j], target))
             gathers[q].append(
                 remote(hb.at[q, z], hb.at[q, z], ag_send.at[q, j], ag_recv.at[q, j], target)
             )
@@ -144,7 +150,11 @@
     def pair_sum(q):
         swaps[q].wait_recv()
         ss[q] = (sp[q, core].astype(F32) + db[q].astype(F32)).astype(BF)
-        sides[q].start()
+        if q in LATE:
+            for copy in scatters[q]:
+                copy.start()
+        else:
+            sides[q].start()
 
     loads[1].wait()
     slab(0, 1)
@@ -167,21 +177,40 @@
     p_out.start()
     p_side.start()
 
-    for q in range(4):
+    for q in sides:
         sides[q].wait_recv()
         su[q] = (ss[q, x_hi].astype(F32) + xb[q].astype(F32)).astype(BF)
         for copy in scatters[q]:
             copy.start()
 
-    for q in range(4):
-        total = su[q, z].astype(F32)
+    def cross(q):
+        i = LATE.index(q)
         for copy in scatters[q]:
             copy.wait_recv()
+        total = ss[q, :, z].astype(F32)
         for j in range(1, 8):
-            total = total + rb[q, j].astype(F32)
+            total = total + rz[i, j].astype(F32)
+        zf[i] = total
+        zb[i] = total.astype(BF)
+        late_sides[q].start()
+
+    def give(q):
+        if q in LATE:
+            late_sides[q].wait_recv()
+            total = zf[LATE.index(q), x_hi] + zx[LATE.index(q)].astype(F32)
+        else:
+            total = su[q, z].astype(F32)
+            for copy in scatters[q]:
+                copy.wait_recv()
+            for j in range(1, 8):
+                total = total + rb[q, j].astype(F32)
         hb[q, z] = total.astype(BF)
         for copy in gathers[q]:
             copy.start()
+
+    for act, q in STEPS:
+        (cross if act == "cross" else give)(q)
+
     p_out.wait_recv()
     p_fwd.start()
 
@@ -274,7 +303,7 @@
     out_ref[16:20, 256:512] = total[4:8, :]
     out_ref[16:20, 512:720] = total[8:12, 0:208]
 
-    for copy in swaps + sides + [p_out, p_side, p_fwd] + mains[:4] + mains[5:] + tails[:4] + tails[5:]:
+    for copy in swaps + list(sides.values()) + list(late_sides.values()) + [p_out, p_side, p_fwd] + mains[:4] + mains[5:] + tails[:4] + tails[5:]:
         copy.wait_send()
     for q in range(4):
         for copy in scatters[q] + gathers[q]:
@@ -307,6 +336,10 @@
             pltpu.VMEM((4, 8, 16, 256), BF),
             pltpu.VMEM((4, 8, 16, 256), BF),
             pltpu.VMEM((4, 8, 16, 256), BF),
+            pltpu.VMEM((len(LATE), 8, 2, 16, 256), BF),
+            pltpu.VMEM((len(LATE), 2, 16, 256), F32),
+            pltpu.VMEM((len(LATE), 2, 16, 256), BF),
+            pltpu.VMEM((len(LATE), 16, 256), BF),
             pltpu.VMEM((4, 8, 16, 256), BF),
             pltpu.VMEM((160, 768), BF),
             pltpu.VMEM((768, 768), BF),

time: 43.5 us -> 42.6 us (0.979)
  Pallas kernels: 41.9 us -> 40.8 us
    pallas_call x1, Pallas kernels: 41.9 us -> 40.8 us  [on_device(): pl.pallas_call(kernel, out_shape=jax.ShapeDtypeStruct((20, 720), F32), in...]
where the time goes in v5:
time: 42.6 us; the launch traced here: 42.3 us
  Pallas kernels  40.8 us (96%)
  local copies, waits for them, and re-layouts  1.52 us (4%)
    pallas_call x1, Pallas kernels, on_device(): pl.pallas_call(kernel, out_shape=jax.ShapeDtypeStruct((20, 720), F32), in...  40.8 us
    unnamed x1, local copies, waits for them, and re-layouts  1.52 us

profile of v5, /device:TPU:2, one launch (start us, length us, event | category | flops | bytes accessed | tf_op | source)
XLA Modules:
  0.0 42.3 jit_solution(13761325884700737479)
XLA Ops:
  0.0 40.8 %shard_map.46 = f32[20,720]{1,0:T(8,128)} custom-call(bf16[2048,80]{1,0:T(8,128)(2,1)} %bitcast.4, bf16[2048,640]{1,0:T(8,128)(2,1)} %bitcast.3, bf16[180,720]{1,0:T(8,128)(2,1)} %bitcast.5, bf16[640,640]{1,0:T(8,128)(2,1)} %o_h.1), custom_call_target="tpu_custom_call" | custom-call | flops 3000000000 | bytes 5000000 | tf_op jit(solution)/shard_map/pallas_call | solution.py:320
  40.8 1.5 %copy.6 = f32[20,720]{1,0:T(8,128)} copy(f32[20,720]{1,0:T(8,128)} %shard_map.46) | data formatting | bytes 115200

commit v6 on v5

--- a/solution.py
+++ b/solution.py
@@ -29,7 +29,7 @@
 def kernel(
     img_h, g_h, p_h, o_h, out_ref,
     img_v, g_v, o_v, o_rows, pbuf, patches, t_v,
-    sp, db, ss, xb, su, rb, rz, zf, zb, zx, hb,
+    own, sp, db, ss, xb, su, rb, rz, zf, zb, zx, hb,
     hmat, pcat, acc, main_out, main_in, tail_out, tail_in,
     load_sem, p_send, p_recv, d_send, d_recv, x_send, x_recv, rs_send, rs_recv, ag_send, ag_recv,
     m_send, m_recv, t_send, t_recv,
@@ -85,16 +85,18 @@
 
     loads[2].wait()
     r = iota((640, 1), 0)
-    rest = r - 512
-    main = r < 512
-    r_core = jnp.where(main, r >> 8, rest >> 6)
-    r_half = jnp.where(main, (r >> 7) & 1, (rest >> 5) & 1)
+    r_core = jnp.where(r < 320, 0, 1)
+    r = r - 320 * r_core
+    rest = r - 256
+    main = r < 256
+    r_half = jnp.where(main, r >> 7, rest >> 5)
     r_own = jnp.where(main, (r >> 4) & 7, (rest >> 2) & 7)
     r_t = jnp.where(main, r & 15, 16 + (rest & 3))
     wanted = 80 * ((r_own + 4) & 7) + 40 * r_half + 20 * r_core + r_t
-    o_rows[...] = dot(one_hot(iota((640, 640), 1) == wanted), o_v[...], ((1,), (0,))).astype(BF)
-
-    def slab(m, kh, between=None):
+    ordered = dot(one_hot(iota((640, 640), 1) == wanted), o_v[...], ((1,), (0,))).astype(BF)
+    o_rows[...] = ordered.reshape(2, 320, 640)
+
+    def slab(kh):
         for kw in range(3):
             if kh == 0:
                 piece = jnp.where(row == 0, zero, pltpu.roll(taps[kw], 32, 1))
@@ -104,22 +106,21 @@
                 piece = jnp.where(row == 31, zero, pltpu.roll(taps[kw], 2016, 1))
             patches[80 * kw : 80 * kw + 80, :] = piece.astype(BF)
         t_v[0:240, :] = dot(patches[...], g_v[...], ((1,), (0,))).astype(BF)
-        if between is not None:
-            pair_sum(between)
-        mixed = dot(o_rows[...], t_v[...], ((1,), (1,))).astype(BF)
-        sp[m] = mixed[0:512].reshape(2, 2, 8, 16, 256)
-        for owner in range(2):
-            for half in range(2):
-                for e in range(2):
-                    top = 512 + 64 * owner + 32 * half + 16 * e
-                    sp[3, owner, half, 3 * e + m] = mixed[top : top + 16]
+
+    def mix(m, side, target):
+        mixed = dot(o_rows[side], t_v[...], ((1,), (1,))).astype(target.dtype)
+        target[m] = mixed[0:256].reshape(2, 8, 16, 256)
+        for half in range(2):
+            for e in range(2):
+                top = 256 + 32 * half + 16 * e
+                target[3, half, 3 * e + m] = mixed[top : top + 16]
 
     def remote(src, dst, send, recv, target):
         return pltpu.make_async_remote_copy(
             src_ref=src, dst_ref=dst, send_sem=send, recv_sem=recv, device_id=target, device_id_type=MESH
         )
 
-    swaps = [remote(sp.at[q, 1 - core], db.at[q], d_send.at[q], d_recv.at[q], sibling) for q in range(4)]
+    swaps = [remote(sp.at[q], db.at[q], d_send.at[q], d_recv.at[q], sibling) for q in range(4)]
     sides = {
         q: remote(
             ss.at[q, 1 - x_hi, pl.ds(0, n)], xb.at[q, pl.ds(0, n)], x_send.at[q], x_recv.at[q], partner
@@ -149,7 +150,7 @@
     p_fwd = remote(pbuf.at[theirs], pbuf.at[theirs], p_send.at[2], p_recv.at[2], sibling)
     def pair_sum(q):
         swaps[q].wait_recv()
-        ss[q] = (sp[q, core].astype(F32) + db[q].astype(F32)).astype(BF)
+        ss[q] = (own[q] + db[q].astype(F32)).astype(BF)
         if q in LATE:
             for copy in scatters[q]:
                 copy.start()
@@ -157,19 +158,26 @@
             sides[q].start()
 
     loads[1].wait()
-    slab(0, 1)
+    slab(1)
+    mix(0, 1 - core, sp)
     pl.semaphore_wait(barrier, 16 + jnp.where(stays, 0, 1))
     swaps[0].start()
-    for owner in range(2):
-        for half in range(2):
-            sp[3, owner, half, 6:8] = jnp.zeros((2, 16, 256), BF)
+    mix(0, core, own)
+    for half in range(2):
+        sp[3, half, 6:8] = jnp.zeros((2, 16, 256), BF)
+        own[3, half, 6:8] = jnp.zeros((2, 16, 256), F32)
     xb[3, 6:8] = jnp.zeros((2, 16, 256), BF)
-    slab(1, 0)
+    slab(0)
+    mix(1, 1 - core, sp)
     swaps[1].start()
     pair_sum(0)
-    slab(2, 2, 1)
+    mix(1, core, own)
+    slab(2)
+    pair_sum(1)
+    mix(2, 1 - core, sp)
     swaps[2].start()
     swaps[3].start()
+    mix(2, core, own)
     pair_sum(2)
     pair_sum(3)
 
@@ -326,11 +334,12 @@
             pltpu.VMEM((2048, 80), BF),
             pltpu.VMEM((2048, 640), BF),
             pltpu.VMEM((640, 640), BF),
-            pltpu.VMEM((640, 640), BF),
+            pltpu.VMEM((2, 320, 640), BF),
             pltpu.VMEM((4, 180, 720), BF),
             pltpu.VMEM((240, 2048), BF),
             pltpu.VMEM((256, 640), BF),
-            pltpu.VMEM((4, 2, 2, 8, 16, 256), BF),
+            pltpu.VMEM((4, 2, 8, 16, 256), F32),
+            pltpu.VMEM((4, 2, 8, 16, 256), BF),
             pltpu.VMEM((4, 2, 8, 16, 256), BF),
             pltpu.VMEM((4, 2, 8, 16, 256), BF),
             pltpu.VMEM((4, 8, 16, 256), BF),

time: 42.6 us -> 42 us (0.986)
  Pallas kernels: 40.8 us -> 40.2 us
    pallas_call x1, Pallas kernels: 40.8 us -> 40.2 us  [on_device(): pl.pallas_call(kernel, out_shape=jax.ShapeDtypeStruct((20, 720), F32), in...]
where the time goes in v6:
time: 42 us; the launch traced here: 41.7 us
  Pallas kernels  40.2 us (96%)
  local copies, waits for them, and re-layouts  1.52 us (4%)
    pallas_call x1, Pallas kernels, on_device(): pl.pallas_call(kernel, out_shape=jax.ShapeDtypeStruct((20, 720), F32), in...  40.2 us
    unnamed x1, local copies, waits for them, and re-layouts  1.52 us

profile of v6, /device:TPU:2, one launch (start us, length us, event | category | flops | bytes accessed | tf_op | source)
XLA Modules:
  0.0 41.7 jit_solution(16614187674322228688)
XLA Ops:
  0.0 40.2 %shard_map.46 = f32[20,720]{1,0:T(8,128)} custom-call(bf16[2048,80]{1,0:T(8,128)(2,1)} %bitcast.4, bf16[2048,640]{1,0:T(8,128)(2,1)} %bitcast.3, bf16[180,720]{1,0:T(8,128)(2,1)} %bitcast.5, bf16[640,640]{1,0:T(8,128)(2,1)} %o_h.1), custom_call_target="tpu_custom_call" | custom-call | flops 3000000000 | bytes 5000000 | tf_op jit(solution)/shard_map/pallas_call | solution.py:328
  40.2 1.5 %copy.6 = f32[20,720]{1,0:T(8,128)} copy(f32[20,720]{1,0:T(8,128)} %shard_map.46) | data formatting | bytes 115200

commit v7 on v6

--- a/solution.py
+++ b/solution.py
@@ -46,12 +46,13 @@
 
     loads = [
         pltpu.make_async_copy(img_h, img_v, load_sem.at[0]),
-        pltpu.make_async_copy(g_h, g_v, load_sem.at[1]),
+        pltpu.make_async_copy(g_h.at[0:1024], g_v.at[0:1024], load_sem.at[1]),
         pltpu.make_async_copy(o_h, o_v, load_sem.at[2]),
         pltpu.make_async_copy(p_h, pbuf.at[low], load_sem.at[3]),
+        pltpu.make_async_copy(g_h.at[1024:2048], g_v.at[1024:2048], load_sem.at[4]),
     ]
-    for load in loads:
-        load.start()
+    for n in (0, 2, 1, 4, 3):
+        loads[n].start()
 
     barrier = pltpu.get_barrier_semaphore()
 
@@ -105,7 +106,11 @@
             else:
                 piece = jnp.where(row == 31, zero, pltpu.roll(taps[kw], 2016, 1))
             patches[80 * kw : 80 * kw + 80, :] = piece.astype(BF)
-        t_v[0:240, :] = dot(patches[...], g_v[...], ((1,), (0,))).astype(BF)
+        product = dot(patches[:, 0:1024], g_v[0:1024], ((1,), (0,)))
+        if kh == 1:
+            loads[4].wait()
+        product = product + dot(patches[:, 1024:2048], g_v[1024:2048], ((1,), (0,)))
+        t_v[0:240, :] = product.astype(BF)
 
     def mix(m, side, target):
         mixed = dot(o_rows[side], t_v[...], ((1,), (1,))).astype(target.dtype)
@@ -357,7 +362,7 @@
             pltpu.VMEM((8, 16, 768), BF),
             pltpu.VMEM((8, 16, 256), BF),
             pltpu.VMEM((8, 16, 256), BF),
-            dma((4,)),
+            dma((5,)),
             dma((3,)), dma((3,)),
             dma((4,)), dma((4,)),
             dma((4,)), dma((4,)),

time: 42 us -> 41.8 us (level)
  no operation moved by 1% of the time
where the time goes in v7:
time: 41.8 us; the launch traced here: 41.4 us
  Pallas kernels  39.8 us (95%)
  local copies, waits for them, and re-layouts  1.52 us (4%)
    pallas_call x1, Pallas kernels, on_device(): pl.pallas_call(kernel, out_shape=jax.ShapeDtypeStruct((20, 720), F32), in...  39.8 us
    unnamed x1, local copies, waits for them, and re-layouts  1.52 us

profile of v7, /device:TPU:2, one launch (start us, length us, event | category | flops | bytes accessed | tf_op | source)
XLA Modules:
  0.0 41.4 jit_solution(14317982076529668799)
XLA Ops:
  0.0 39.8 %shard_map.46 = f32[20,720]{1,0:T(8,128)} custom-call(bf16[2048,80]{1,0:T(8,128)(2,1)} %bitcast.4, bf16[2048,640]{1,0:T(8,128)(2,1)} %bitcast.3, bf16[180,720]{1,0:T(8,128)(2,1)} %bitcast.5, bf16[640,640]{1,0:T(8,128)(2,1)} %o_h.1), custom_call_target="tpu_custom_call" | custom-call | flops 3000000000 | bytes 5000000 | tf_op jit(solution)/shard_map/pallas_call | solution.py:333
  39.8 1.5 %copy.6 = f32[20,720]{1,0:T(8,128)} copy(f32[20,720]{1,0:T(8,128)} %shard_map.46) | data formatting | bytes 115200

commit v8 on v7

--- a/solution.py
+++ b/solution.py
@@ -187,11 +187,12 @@
     pair_sum(3)
 
     loads[3].wait()
-    p_out.start()
-    p_side.start()
 
     for q in sides:
         sides[q].wait_recv()
+        if q == 1:
+            p_out.start()
+            p_side.start()
         su[q] = (ss[q, x_hi].astype(F32) + xb[q].astype(F32)).astype(BF)
         for copy in scatters[q]:
             copy.start()

time: 41.8 us -> 42 us (level)
  no operation moved by 1% of the time
where the time goes in v8:
time: 42 us; the launch traced here: 41.2 us
  Pallas kernels  39.7 us (95%)
  local copies, waits for them, and re-layouts  1.52 us (4%)
    pallas_call x1, Pallas kernels, on_device(): pl.pallas_call(kernel, out_shape=jax.ShapeDtypeStruct((20, 720), F32), in...  39.7 us
    unnamed x1, local copies, waits for them, and re-layouts  1.52 us

profile of v8, /device:TPU:2, one launch (start us, length us, event | category | flops | bytes accessed | tf_op | source)
XLA Modules:
  0.0 41.2 jit_solution(13369877560715075383)
XLA Ops:
  0.0 39.7 %shard_map.46 = f32[20,720]{1,0:T(8,128)} custom-call(bf16[2048,80]{1,0:T(8,128)(2,1)} %bitcast.4, bf16[2048,640]{1,0:T(8,128)(2,1)} %bitcast.3, bf16[180,720]{1,0:T(8,128)(2,1)} %bitcast.5, bf16[640,640]{1,0:T(8,128)(2,1)} %o_h.1), custom_call_target="tpu_custom_call" | custom-call | flops 3000000000 | bytes 5000000 | tf_op jit(solution)/shard_map/pallas_call | solution.py:334
  39.7 1.5 %copy.6 = f32[20,720]{1,0:T(8,128)} copy(f32[20,720]{1,0:T(8,128)} %shard_map.46) | data formatting | bytes 115200
